TPU v7x, 32 devices: a whole 2x2x4 slice. The times are simulated.
32 devices in a mesh: bx: 8 (over z, y), by: 4 (over x, core).
Axes of the slice: x: 2, y: 2, z: 4, core: 2. Of those that a mesh axis runs over, the one named last changes fastest.
Arguments:
- source: bfloat16 [8, 4, 2, 128, 1024], P('bx', 'by'), may hold values from -6 to 6
- start_tick: int32 [8, 4], P('bx', 'by'), may hold values from 0 to 3, as said below
- op_x: bfloat16 [8, 4, 2, 1024, 1024], P('bx', 'by'), may hold values from -0.09375 to 0.09375
- op_y: bfloat16 [8, 4, 2, 1024, 1024], P('bx', 'by'), may hold values from -0.09375 to 0.09375
Outputs:
- upgoing: float32 [4, 128, 2, 8, 1024], P('by', 'bx')
Inputs may be any that keep to these rules, and one draw needn't show every extreme that they name: `start_tick`: both 0 and 3 occur in every draw.
All inputs are finite; a program needn't handle non-finite values.
Results may differ from a plain program's by a relative error of at most 0.012.
Values may be sent and summed in bfloat16 or wider, within the bound.
A program may use at most 64 MiB of HBM per device.

v0:
```python
import functools
import math

import jax
import jax.numpy as jnp
import ml_dtypes
import numpy as np
from jax import lax
from jax.experimental import pallas as pl
from jax.experimental.pallas import tpu as pltpu
from jax.sharding import PartitionSpec as P

TICKS = 4
CHUNKS = 2
MESH = pl.DeviceIdType.MESH
BF16 = jnp.bfloat16
F32 = jnp.float32


def dft_tables(length):
    indices = np.arange(length, dtype=np.int64)
    angles = (indices[:, None] * indices[None, :] % length) * (2.0 * math.pi / length)
    return np.cos(angles).astype(ml_dtypes.bfloat16), np.sin(angles).astype(ml_dtypes.bfloat16)


def grid_gain(pieces):
    wave = np.arange(pieces)
    signed = np.where(wave < pieces // 2, wave, wave - pieces).astype(np.float64)
    return (0.5 * (1.0 + signed / np.sqrt(signed * signed + 1.0))).astype(np.float32)


def grid_matrix(pieces, owned):
    cos_grid, sin_grid = (t.astype(np.float32) for t in dft_tables(pieces))
    parts = np.zeros((2, pieces, pieces, 2), np.float32)
    parts[0, :, :, 0] = cos_grid.T
    parts[0, :, :, 1] = sin_grid.T
    parts[1, :, :, 0] = -sin_grid.T
    parts[1, :, :, 1] = cos_grid.T
    full = np.einsum("cqir,st->scqirt", parts, np.eye(owned, dtype=np.float32))
    side = 2 * pieces * owned
    return full.reshape(side, side).astype(ml_dtypes.bfloat16)


def kernel(
    plan,
    first_ref, source_hbm, opx_hbm, opy_hbm, tables_hbm,
    out_ref,
    source_ref, opx, opy, tables, left, e_out, n_out, e_in, n_in, relay_in, d_out, d_in, nf_in, nb_in, spec, regroup,
    load_sem, e_send, e_recv, n_send, n_recv, r_send, r_recv, d_send, d_recv,
    nf_send, nf_recv, nb_send, nb_recv, s_send, s_recv,
):
    pieces, rows_by, per, group, fused = plan
    chunks = CHUNKS
    half = per * group
    width = source_hbm.shape[2]
    tile = min(256, width)
    i, j = lax.axis_index("bx"), lax.axis_index("by")
    odd = lax.rem(i, 2)
    partner = i + 1 - 2 * odd
    relay_to = i - 2 + 4 * odd
    relay_from = i + 2 - 4 * odd
    has_relay_to = (relay_to >= 0) & (relay_to < pieces)
    has_relay_from = (relay_from >= 0) & (relay_from < pieces)

    starts = range(0, width, tile)

    def load(src, dst, k):
        return pltpu.make_async_copy(src, dst, load_sem.at[k])

    def by_tiles(src, dst, k):
        return [
            load(src.at[:, start : start + tile], dst.at[:, start : start + tile], k + n)
            for n, start in enumerate(starts)
        ]

    count = len(starts)
    source_load = load(source_hbm, source_ref, 0)
    opx_loads = by_tiles(opx_hbm, opx, 1)
    opy_loads = by_tiles(opy_hbm, opy, 1 + count)
    tables_load = load(tables_hbm, tables, 1 + 2 * count)
    for copy in [source_load, *opx_loads, *opy_loads]:
        copy.start()

    barrier = pltpu.get_barrier_semaphore()
    for k in range(1, pieces):
        pl.semaphore_signal(
            barrier, inc=1, device_id={"bx": lax.rem(i + k, pieces)}, device_id_type=MESH
        )

    @pl.when(j > 0)
    def _():
        pl.semaphore_signal(barrier, inc=1, device_id={"by": j - 1}, device_id_type=MESH)

    @pl.when(j < rows_by - 1)
    def _():
        pl.semaphore_signal(barrier, inc=1, device_id={"by": j + 1}, device_id_type=MESH)

    def clear(ref, tick, c):
        ref[tick, c] = jnp.zeros(ref.shape[2:], ref.dtype)

    def clear_all(c, _):
        clear(e_in, 0, c)
        clear(n_in, 0, c)

        @pl.when(i == 0)
        def _():
            for tick in range(1, TICKS):
                clear(e_in, tick, c)

        @pl.when(j == 0)
        def _():
            for tick in range(1, TICKS):
                clear(n_in, tick, c)
            nf_in[c] = jnp.zeros(nf_in.shape[1:], BF16)

        @pl.when(j == rows_by - 1)
        def _():
            nb_in[c] = jnp.zeros(nb_in.shape[1:], BF16)

        @pl.when(jnp.logical_not(has_relay_from))
        def _():
            relay_in[c] = jnp.zeros(relay_in.shape[1:], BF16)

        return 0

    lax.fori_loop(0, chunks, clear_all, 0)

    peers = pieces - 1 + (j > 0).astype(jnp.int32) + (j < rows_by - 1).astype(jnp.int32)
    pl.semaphore_wait(barrier, peers)

    def remote(src, dst, send, recv, where):
        return pltpu.make_async_remote_copy(
            src_ref=src, dst_ref=dst, send_sem=send, recv_sem=recv, device_id=where, device_id_type=MESH
        )

    def east(tick, c):
        return remote(
            e_out.at[tick, c], e_in.at[tick + 1, c], e_send.at[tick, c], e_recv.at[tick, c], {"bx": i + 1}
        )

    def north(tick, c):
        return remote(
            n_out.at[tick, c], n_in.at[tick + 1, c], n_send.at[tick, c], n_recv.at[tick, c], {"by": j + 1}
        )

    def relay(c):
        return remote(
            e_out.at[TICKS - 1, c], relay_in.at[c], r_send.at[c], r_recv.at[c], {"bx": relay_to}
        )

    def difference(c):
        return remote(d_out.at[c], d_in.at[c], d_send.at[c], d_recv.at[c], {"bx": partner})

    def final_north(c):
        return remote(n_out.at[TICKS - 1, c], nf_in.at[c], nf_send.at[c], nf_recv.at[c], {"by": j + 1})

    def final_south(c):
        return remote(n_out.at[TICKS - 1, c], nb_in.at[c], nb_send.at[c], nb_recv.at[c], {"by": j - 1})

    def owner(c, o):
        if o % 2 == 1 and chunks % 2 == 0:
            return c + 1 - 2 * lax.rem(c, 2) + chunks * o
        return c + chunks * o

    def regrouped(c, o):
        return remote(
            spec.at[c, o], regroup.at[i], s_send.at[c, o], s_recv.at[i], {"bx": owner(c, o)}
        )

    def shot_rows(c, o):
        return pl.ds(pl.multiple_of(owner(c, o) * group, group), group)

    def place(part, at, size, value):
        if part == 0:
            left[at : at + size, :width] = value
            left[half + at : half + at + size, width:] = value
        else:
            left[at : at + size, width:] = -value
            left[half + at : half + at + size, :width] = value

    def product(matrix, put, loads=None, first=None, depth=None):
        for n, start in enumerate(starts):
            cols = slice(start, start + tile)
            if loads is not None:
                pl.when(first)(loads[n].wait)
            got = jnp.dot(left[...], matrix[:depth, cols], preferred_element_type=F32)
            put(cols, got.astype(BF16))

    def incident(tick, c):
        active = (first_ref[0, 0] <= tick).astype(F32)
        for part in range(2):
            for o in range(per):
                at = o * group
                rows = slice(part * half + at, part * half + at + group)
                value = (
                    e_in[tick, c, rows, :].astype(F32)
                    + n_in[tick, c, rows, :].astype(F32)
                    + active * source_ref[part, shot_rows(c, o), :].astype(F32)
                )
                place(part, at, group, value.astype(BF16))

    def arrive(tick, c):
        @pl.when(i > 0)
        def _():
            east(tick - 1, c).wait_recv()

        @pl.when(j > 0)
        def _():
            north(tick - 1, c).wait_recv()

    def sweep(step, _):
        tick, c = step // chunks, lax.rem(step, chunks)

        @pl.when(tick > 0)
        def _():
            arrive(tick, c)

        incident(tick, c)

        def put_east(cols, value):
            e_out[tick, c, :, cols] = value

        product(opx, put_east, opx_loads, step == 0)

        @pl.when(i < pieces - 1)
        def _():
            east(tick, c).start()

        def put_north(cols, value):
            n_out[tick, c, :, cols] = value

        product(opy, put_north, opy_loads, step == 0)

        @pl.when(j < rows_by - 1)
        def _():
            north(tick, c).start()

        return 0

    source_load.wait()
    lax.fori_loop(0, chunks, sweep, 0)
    tables_load.start()
    lax.fori_loop(chunks, (TICKS - 1) * chunks, sweep, 0)
    tables_load.wait()
    last = TICKS - 1

    def last_tick(c):
        arrive(last, c)
        incident(last, c)

        def put_east(cols, value):
            e_out[last, c, :, cols] = value

        product(opx, put_east)

        @pl.when(has_relay_to)
        def _():
            relay(c).start()

        def put_north(cols, value):
            n_out[last, c, :, cols] = value

        product(opy, put_north)

        @pl.when(j < rows_by - 1)
        def _():
            final_north(c).start()

        @pl.when(j > 0)
        def _():
            final_south(c).start()

    def subtract(c):
        @pl.when(has_relay_from)
        def _():
            relay(c).wait_recv()

        sign = (2 * odd - 1).astype(F32)
        d_out[c] = (sign * (relay_in[c].astype(F32) - e_out[last, c].astype(F32))).astype(BF16)
        difference(c).start()

    def reflect(c):
        difference(c).wait_recv()

        @pl.when(j > 0)
        def _():
            final_north(c).wait_recv()

        @pl.when(j < rows_by - 1)
        def _():
            final_south(c).wait_recv()

        for part in range(2):
            rows = slice(part * half, (part + 1) * half)
            value = (
                d_in[c, rows, :].astype(F32) + nf_in[c, rows, :].astype(F32) - nb_in[c, rows, :].astype(F32)
            )
            place(part, 0, half, value.astype(BF16))

        def put_reflected(cols, value):
            d_out_free[:, cols] = value

        d_out_free = e_in.at[0, c]
        product(opx, put_reflected)
        for part in range(2):
            place(part, 0, half, d_out_free[part * half : (part + 1) * half, :])

        def put_spectrum(cols, value):
            for part in range(2):
                for o in range(per):
                    at = part * half + o * group
                    if fused:
                        spec[c, o, part * group : (part + 1) * group, cols] = value[at : at + group]
                    else:
                        out_ref[part, shot_rows(c, o), cols] = value[at : at + group]

        product(tables, put_spectrum, depth=2 * width)
        if fused:
            for o in range(per):
                @pl.when(owner(c, o) == i)
                def _():
                    regroup[i] = spec[c, o]

                @pl.when(owner(c, o) != i)
                def _():
                    regrouped(c, o).start()

    def finish(step, _):
        @pl.when(step < chunks)
        def _():
            last_tick(step)

        @pl.when((step >= 1) & (step <= chunks))
        def _():
            subtract(step - 1)

        @pl.when(step >= 2)
        def _():
            reflect(step - 2)

        return 0

    lax.fori_loop(0, chunks + 2, finish, 0)

    def sent(c, _):
        for tick in range(TICKS - 1):
            @pl.when(i < pieces - 1)
            def _():
                east(tick, c).wait_send()

            @pl.when(j < rows_by - 1)
            def _():
                north(tick, c).wait_send()

        @pl.when(has_relay_to)
        def _():
            relay(c).wait_send()

        @pl.when(j < rows_by - 1)
        def _():
            final_north(c).wait_send()

        @pl.when(j > 0)
        def _():
            final_south(c).wait_send()

        difference(c).wait_send()
        return 0

    lax.fori_loop(0, chunks, sent, 0)

    if fused:
        for k in range(1, pieces):
            peer = lax.rem(i + k, pieces)
            remote(
                spec.at[0, 0], regroup.at[peer], s_send.at[0, 0], s_recv.at[peer], {"bx": peer}
            ).wait_recv()
        side = 2 * pieces * group
        whole = regroup[...].reshape(side, width)
        wave = lax.rem(lax.broadcasted_iota(jnp.int32, (side, tile), 0), pieces)
        signed = jnp.where(wave < pieces // 2, wave, wave - pieces).astype(F32)
        gain = 0.5 * (1.0 + signed / jnp.sqrt(signed * signed + 1.0))
        for start in range(0, width, tile):
            cols = slice(start, start + tile)
            got = jnp.dot(tables[2 * width :, :side], whole[:, cols], preferred_element_type=F32)
            out_ref[:, cols] = got * gain
        for c in range(chunks):
            for o in range(per):
                @pl.when(owner(c, o) != i)
                def _():
                    regrouped(c, o).wait_send()


def shards(source, start_tick, op_x, op_y):
    pieces, rows_by = lax.axis_size("bx"), lax.axis_size("by")
    _, _, _, shots, width = source.shape
    owned = shots // pieces
    fused = owned % 16 == 0 and pieces % CHUNKS == 0 and 2 * shots <= width
    per, group = (pieces // CHUNKS, owned) if fused else (1, shots // CHUNKS)
    rows = 2 * per * group
    side = 2 * pieces * owned

    cos_line, sin_line = dft_tables(width)
    tables = np.concatenate([cos_line, -sin_line])
    if fused:
        grid = np.zeros((side, width), ml_dtypes.bfloat16)
        grid[:, :side] = grid_matrix(pieces, owned)
        tables = np.concatenate([tables, grid])
    tables = jnp.asarray(tables)

    out_shape = (
        jax.ShapeDtypeStruct((side, width), F32) if fused else jax.ShapeDtypeStruct((2, shots, width), BF16)
    )
    ticked = pltpu.VMEM((TICKS, CHUNKS, rows, width), BF16)
    single = pltpu.VMEM((CHUNKS, rows, width), BF16)
    operator = pltpu.VMEM((2 * width, width), BF16)
    ticked_sem = pltpu.SemaphoreType.DMA((TICKS - 1, CHUNKS))
    single_sem = pltpu.SemaphoreType.DMA((CHUNKS,))
    result = pl.pallas_call(
        functools.partial(kernel, (pieces, rows_by, per, group, fused)),
        out_shape=out_shape,
        in_specs=[pl.BlockSpec(memory_space=pltpu.SMEM)] + [pl.BlockSpec(memory_space=pl.ANY)] * 4,
        out_specs=pl.BlockSpec(memory_space=pltpu.VMEM),
        scratch_shapes=[
            pltpu.VMEM((2, shots, width), BF16),
            operator, operator,
            pltpu.VMEM(tables.shape, BF16),
            pltpu.VMEM((rows, 2 * width), BF16),
            ticked, ticked, ticked, ticked,
            single, single, single, single, single,
            pltpu.VMEM((CHUNKS, per, 2 * group, width), BF16),
            pltpu.VMEM((pieces, 2 * group, width) if fused else (1, 16, 128), BF16),
            pltpu.SemaphoreType.DMA((2 + 2 * pl.cdiv(width, 256),)),
            ticked_sem, ticked_sem, ticked_sem, ticked_sem,
            single_sem, single_sem, single_sem, single_sem,
            single_sem, single_sem, single_sem, single_sem,
            pltpu.SemaphoreType.DMA((CHUNKS, per)),
            pltpu.SemaphoreType.DMA((pieces,)),
        ],
        compiler_params=pltpu.CompilerParams(
            collective_id=0, has_side_effects=True, vmem_limit_bytes=60 * 1024 * 1024
        ),
        cost_estimate=pl.CostEstimate(
            flops=2 * rows * CHUNKS * 2 * width * width * 10, bytes_accessed=16 * width * width, transcendentals=0
        ),
    )(
        start_tick,
        source[0, 0],
        op_x.reshape(2 * width, width),
        op_y.reshape(2 * width, width),
        tables,
    )
    if fused:
        return result.reshape(1, owned, 2, pieces, width)
    arranged = result.reshape(2, pieces, owned, 1, width)
    spectrum = lax.all_to_all(arranged, "bx", split_axis=1, concat_axis=3, tiled=True)
    received = spectrum.reshape(2, owned, pieces, width)
    cos_grid, sin_grid = (jnp.asarray(t) for t in dft_tables(pieces))

    def over_grid(values, table):
        return jnp.einsum("sik,iq->sqk", values, table, preferred_element_type=F32)

    out_real = over_grid(received[0], cos_grid) + over_grid(received[1], sin_grid)
    out_imag = over_grid(received[1], cos_grid) - over_grid(received[0], sin_grid)
    upgoing = jnp.stack([out_real, out_imag], axis=1) * grid_gain(pieces)[None, None, :, None]
    return upgoing[None]


def solution(mesh):
    placed = (
        P("bx", "by", None, None, None),
        P("bx", "by"),
        P("bx", "by", None, None, None),
        P("bx", "by", None, None, None),
    )
    return jax.shard_map(
        shards,
        mesh=mesh,
        in_specs=placed,
        out_specs=P("by", "bx", None, None, None),
        check_vma=False,
    )
```

profile of v0, /device:TPU:4, one launch (start us, length us, event | category | flops | bytes accessed | tf_op | source)
XLA Modules:
  0.0 74.2 jit_solution(9812331104480285784)
XLA Ops:
  0.7 71.2 %shard_map.55 = f32[256,1024]{1,0:T(8,128)} custom-call(s32[1,1]{1,0:T(1,128)S(6)} %copy.7.first_ref, bf16[2,128,1024]{2,1,0:T(8,128)(2,1)} %bitcast.7, bf16[2048,1024]{1,0:T(8,128)(2,1)} %bitcast.5, bf16[2048,1024]{1,0:T(8,128)(2,1)} %bitcast.6, bf16[2304,1024]{1,0:T(8,128)(2,1)} %constant.2.clone.tables_hbm), custom_call_target="tpu_custom_call" | custom-call | flops 10737418240 | bytes 16777216 | tf_op jit(solution)/shard_map/pallas_call | solution.py:419
  71.9 2.3 %copy.8 = f32[1,16,2,8,1024]{4,3,2,1,0:T(8,128)} copy(f32[1,16,2,8,1024]{4,3,2,1,0:T(8,128)} %bitcast.4) | data formatting | bytes 2097152
where the time goes:
time: 74.4 us; the launch traced here: 74.2 us
  Pallas kernels  71.2 us (96%)
  local copies, waits for them, and re-layouts  2.31 us (3%)
    pallas_call x1, Pallas kernels, shards(): pl.pallas_call(functools.partial(kernel, (pieces, rows_by, per, group, fu...  71.2 us
    unnamed x1, local copies, waits for them, and re-layouts  2.31 us

commit v1 on v0

--- a/solution.py
+++ b/solution.py
@@ -178,12 +178,12 @@
             left[at : at + size, width:] = -value
             left[half + at : half + at + size, :width] = value
 
-    def product(matrix, put, loads=None, first=None, depth=None):
+    def product(matrix, put, loads=None):
         for n, start in enumerate(starts):
             cols = slice(start, start + tile)
             if loads is not None:
-                pl.when(first)(loads[n].wait)
-            got = jnp.dot(left[...], matrix[:depth, cols], preferred_element_type=F32)
+                loads[n].wait()
+            got = jnp.dot(left[...], matrix[:, cols], preferred_element_type=F32)
             put(cols, got.astype(BF16))
 
     def incident(tick, c):
@@ -208,19 +208,20 @@
         def _():
             north(tick - 1, c).wait_recv()
 
-    def sweep(step, _):
-        tick, c = step // chunks, lax.rem(step, chunks)
-
-        @pl.when(tick > 0)
-        def _():
-            arrive(tick, c)
+    def sweep(step, _, first=False):
+        tick, c = (0, 0) if first else (step // chunks, lax.rem(step, chunks))
+
+        if not first:
+            @pl.when(tick > 0)
+            def _():
+                arrive(tick, c)
 
         incident(tick, c)
 
         def put_east(cols, value):
             e_out[tick, c, :, cols] = value
 
-        product(opx, put_east, opx_loads, step == 0)
+        product(opx, put_east, opx_loads if first else None)
 
         @pl.when(i < pieces - 1)
         def _():
@@ -229,7 +230,7 @@
         def put_north(cols, value):
             n_out[tick, c, :, cols] = value
 
-        product(opy, put_north, opy_loads, step == 0)
+        product(opy, put_north, opy_loads if first else None)
 
         @pl.when(j < rows_by - 1)
         def _():
@@ -238,9 +239,9 @@
         return 0
 
     source_load.wait()
-    lax.fori_loop(0, chunks, sweep, 0)
+    sweep(0, 0, first=True)
     tables_load.start()
-    lax.fori_loop(chunks, (TICKS - 1) * chunks, sweep, 0)
+    lax.fori_loop(1, (TICKS - 1) * chunks, sweep, 0)
     tables_load.wait()
     last = TICKS - 1
 
@@ -314,7 +315,7 @@
                     else:
                         out_ref[part, shot_rows(c, o), cols] = value[at : at + group]
 
-        product(tables, put_spectrum, depth=2 * width)
+        product(tables, put_spectrum)
         if fused:
             for o in range(per):
                 @pl.when(owner(c, o) == i)
@@ -375,15 +376,7 @@
             remote(
                 spec.at[0, 0], regroup.at[peer], s_send.at[0, 0], s_recv.at[peer], {"bx": peer}
             ).wait_recv()
-        side = 2 * pieces * group
-        whole = regroup[...].reshape(side, width)
-        wave = lax.rem(lax.broadcasted_iota(jnp.int32, (side, tile), 0), pieces)
-        signed = jnp.where(wave < pieces // 2, wave, wave - pieces).astype(F32)
-        gain = 0.5 * (1.0 + signed / jnp.sqrt(signed * signed + 1.0))
-        for start in range(0, width, tile):
-            cols = slice(start, start + tile)
-            got = jnp.dot(tables[2 * width :, :side], whole[:, cols], preferred_element_type=F32)
-            out_ref[:, cols] = got * gain
+        out_ref[...] = regroup[...]
         for c in range(chunks):
             for o in range(per):
                 @pl.when(owner(c, o) != i)
@@ -395,21 +388,16 @@
     pieces, rows_by = lax.axis_size("bx"), lax.axis_size("by")
     _, _, _, shots, width = source.shape
     owned = shots // pieces
-    fused = owned % 16 == 0 and pieces % CHUNKS == 0 and 2 * shots <= width
+    fused = owned % 16 == 0 and pieces % CHUNKS == 0
     per, group = (pieces // CHUNKS, owned) if fused else (1, shots // CHUNKS)
     rows = 2 * per * group
     side = 2 * pieces * owned
 
     cos_line, sin_line = dft_tables(width)
-    tables = np.concatenate([cos_line, -sin_line])
-    if fused:
-        grid = np.zeros((side, width), ml_dtypes.bfloat16)
-        grid[:, :side] = grid_matrix(pieces, owned)
-        tables = np.concatenate([tables, grid])
-    tables = jnp.asarray(tables)
+    tables = jnp.asarray(np.concatenate([cos_line, -sin_line]))
 
     out_shape = (
-        jax.ShapeDtypeStruct((side, width), F32) if fused else jax.ShapeDtypeStruct((2, shots, width), BF16)
+        jax.ShapeDtypeStruct((pieces, 2 * owned, width), BF16) if fused else jax.ShapeDtypeStruct((2, shots, width), BF16)
     )
     ticked = pltpu.VMEM((TICKS, CHUNKS, rows, width), BF16)
     single = pltpu.VMEM((CHUNKS, rows, width), BF16)
@@ -451,7 +439,10 @@
         tables,
     )
     if fused:
-        return result.reshape(1, owned, 2, pieces, width)
+        grid = jnp.asarray(grid_matrix(pieces, owned))
+        gain = jnp.asarray(np.tile(grid_gain(pieces), 2 * owned))
+        upgoing = jnp.dot(grid, result.reshape(side, width), preferred_element_type=F32) * gain[:, None]
+        return upgoing.reshape(1, owned, 2, pieces, width)
     arranged = result.reshape(2, pieces, owned, 1, width)
     spectrum = lax.all_to_all(arranged, "bx", split_axis=1, concat_axis=3, tiled=True)
     received = spectrum.reshape(2, owned, pieces, width)

time: 74.4 us -> 74 us (level)
  matrix products: 0 us -> 2.32 us
  local copies, waits for them, and re-layouts: 2.31 us -> 0.01 us
    dot_general x0 -> x1, matrix products: none -> 2.32 us  [shards(): jnp.dot(grid, result.reshape(side, width), preferred_element_type=F32)]
    unnamed x1 -> x4, local copies, waits for them, and re-layouts: 2.31 us -> 0.01 us
where the time goes in v1:
time: 74 us; the launch traced here: 73.8 us
  Pallas kernels  70.8 us (96%)
  matrix products  2.32 us (3%)
    pallas_call x1, Pallas kernels, shards(): pl.pallas_call(functools.partial(kernel, (pieces, rows_by, per, group, fu...  70.8 us
    dot_general x1, matrix products, shards(): jnp.dot(grid, result.reshape(side, width), preferred_element_type=F32)  2.32 us

profile of v1, /device:TPU:4, one launch (start us, length us, event | category | flops | bytes accessed | tf_op | source)
XLA Modules:
  0.0 73.8 jit_solution(5103034896776221353)
XLA Ops:
  0.7 0.0 copy-start
  0.7 0.0 copy-start.1
  0.7 70.8 %shard_map.73 = bf16[8,32,1024]{2,1,0:T(8,128)(2,1)} custom-call(s32[1,1]{1,0:T(1,128)S(6)} %copy.8.first_ref, bf16[2,128,1024]{2,1,0:T(8,128)(2,1)} %bitcast.12, bf16[2048,1024]{1,0:T(8,128)(2,1)} %bitcast.10, bf16[2048,1024]{1,0:T(8,128)(2,1)} %bitcast.11, bf16[2048,1024]{1,0:T(8,128)(2,1)} %constant.6.clone.tables_hbm), custom_call_target="tpu_custom_call" | custom-call | flops 10737418240 | bytes 16777216 | tf_op jit(solution)/shard_map/pallas_call | solution.py:407
  71.5 0.0 copy-done
  71.5 0.0 copy-done.1
  71.5 2.3 %convolution_multiply_fusion = f32[1024,256]{0,1:T(8,128)} fusion(bf16[256,256]{1,0:T(8,128)(2,1)S(1)} %copy-done, bf16[256,1024]{1,0:T(8,128)(2,1)} %bitcast.9, f32[256]{0:T(256)S(1)} %copy-done.1), kind=kOutput, calls=%fused_computation | convolution fusion | flops 134479872 | bytes 1704960 | tf_op jit(solution)/shard_map/dot_general | solution.py:444
Async XLA Ops:
  0.7 70.8 %copy-start = (bf16[256,256]{1,0:T(8,128)(2,1)S(1)}, bf16[256,256]{1,0:T(8,128)(2,1)}, u32[]{:S(2)}) copy-start(bf16[256,256]{1,0:T(8,128)(2,1)} %constant.7.clone) | copy-start | bytes 393220
  0.7 70.8 %copy-start.1 = (f32[256]{0:T(256)S(1)}, f32[256]{0:T(256)}, u32[]{:S(2)}) copy-start(f32[256]{0:T(256)} %constant.8.clone) | copy-start | bytes 3076

commit v2 on v1

--- a/solution.py
+++ b/solution.py
@@ -49,7 +49,7 @@
     load_sem, e_send, e_recv, n_send, n_recv, r_send, r_recv, d_send, d_recv,
     nf_send, nf_recv, nb_send, nb_recv, s_send, s_recv,
 ):
-    pieces, rows_by, per, group, fused = plan
+    pieces, rows_by, per, group, fused, spans = plan
     chunks = CHUNKS
     half = per * group
     width = source_hbm.shape[2]
@@ -74,6 +74,7 @@
         ]
 
     count = len(starts)
+    span = width // spans
     source_load = load(source_hbm, source_ref, 0)
     opx_loads = by_tiles(opx_hbm, opx, 1)
     opy_loads = by_tiles(opy_hbm, opy, 1 + count)
@@ -143,13 +144,18 @@
             n_out.at[tick, c], n_in.at[tick + 1, c], n_send.at[tick, c], n_recv.at[tick, c], {"by": j + 1}
         )
 
-    def relay(c):
+    def relay(c, n):
+        cols = pl.ds(starts[n], tile)
         return remote(
-            e_out.at[TICKS - 1, c], relay_in.at[c], r_send.at[c], r_recv.at[c], {"bx": relay_to}
-        )
-
-    def difference(c):
-        return remote(d_out.at[c], d_in.at[c], d_send.at[c], d_recv.at[c], {"bx": partner})
+            e_out.at[TICKS - 1, c, :, cols], relay_in.at[c, :, cols], r_send.at[c, n], r_recv.at[c, n],
+            {"bx": relay_to},
+        )
+
+    def difference(c, n):
+        cols = pl.ds(starts[n], tile)
+        return remote(
+            d_out.at[c, :, cols], d_in.at[c, :, cols], d_send.at[c, n], d_recv.at[c, n], {"bx": partner}
+        )
 
     def final_north(c):
         return remote(n_out.at[TICKS - 1, c], nf_in.at[c], nf_send.at[c], nf_recv.at[c], {"by": j + 1})
@@ -162,9 +168,11 @@
             return c + 1 - 2 * lax.rem(c, 2) + chunks * o
         return c + chunks * o
 
-    def regrouped(c, o):
+    def regrouped(c, o, part):
+        cols = pl.ds(part * span, span)
         return remote(
-            spec.at[c, o], regroup.at[i], s_send.at[c, o], s_recv.at[i], {"bx": owner(c, o)}
+            spec.at[c, o, :, cols], regroup.at[i, :, cols], s_send.at[c, o, part], s_recv.at[i, part],
+            {"bx": owner(c, o)},
         )
 
     def shot_rows(c, o):
@@ -178,13 +186,15 @@
             left[at : at + size, width:] = -value
             left[half + at : half + at + size, :width] = value
 
-    def product(matrix, put, loads=None):
+    def product(matrix, put, loads=None, then=None):
         for n, start in enumerate(starts):
             cols = slice(start, start + tile)
             if loads is not None:
                 loads[n].wait()
             got = jnp.dot(left[...], matrix[:, cols], preferred_element_type=F32)
             put(cols, got.astype(BF16))
+            if then is not None:
+                then(n)
 
     def incident(tick, c):
         active = (first_ref[0, 0] <= tick).astype(F32)
@@ -252,11 +262,12 @@
         def put_east(cols, value):
             e_out[last, c, :, cols] = value
 
-        product(opx, put_east)
-
-        @pl.when(has_relay_to)
-        def _():
-            relay(c).start()
+        def send_east(n):
+            @pl.when(has_relay_to)
+            def _():
+                relay(c, n).start()
+
+        product(opx, put_east, then=send_east)
 
         def put_north(cols, value):
             n_out[last, c, :, cols] = value
@@ -272,16 +283,20 @@
             final_south(c).start()
 
     def subtract(c):
-        @pl.when(has_relay_from)
-        def _():
-            relay(c).wait_recv()
-
         sign = (2 * odd - 1).astype(F32)
-        d_out[c] = (sign * (relay_in[c].astype(F32) - e_out[last, c].astype(F32))).astype(BF16)
-        difference(c).start()
+        for n, start in enumerate(starts):
+            @pl.when(has_relay_from)
+            def _():
+                relay(c, n).wait_recv()
+
+            cols = slice(start, start + tile)
+            value = relay_in[c, :, cols].astype(F32) - e_out[last, c, :, cols].astype(F32)
+            d_out[c, :, cols] = (sign * value).astype(BF16)
+            difference(c, n).start()
 
     def reflect(c):
-        difference(c).wait_recv()
+        for n in range(count):
+            difference(c, n).wait_recv()
 
         @pl.when(j > 0)
         def _():
@@ -315,16 +330,21 @@
                     else:
                         out_ref[part, shot_rows(c, o), cols] = value[at : at + group]
 
-        product(tables, put_spectrum)
-        if fused:
+        def send_spectrum(n):
+            if not fused or (n + 1) * spans % count:
+                return
+            part = (n + 1) * spans // count - 1
+            cols = slice(part * span, (part + 1) * span)
             for o in range(per):
                 @pl.when(owner(c, o) == i)
                 def _():
-                    regroup[i] = spec[c, o]
+                    regroup[i, :, cols] = spec[c, o, :, cols]
 
                 @pl.when(owner(c, o) != i)
                 def _():
-                    regrouped(c, o).start()
+                    regrouped(c, o, part).start()
+
+        product(tables, put_spectrum, then=send_spectrum)
 
     def finish(step, _):
         @pl.when(step < chunks)
@@ -353,9 +373,12 @@
             def _():
                 north(tick, c).wait_send()
 
-        @pl.when(has_relay_to)
-        def _():
-            relay(c).wait_send()
+        for n in range(count):
+            @pl.when(has_relay_to)
+            def _():
+                relay(c, n).wait_send()
+
+            difference(c, n).wait_send()
 
         @pl.when(j < rows_by - 1)
         def _():
@@ -365,7 +388,6 @@
         def _():
             final_south(c).wait_send()
 
-        difference(c).wait_send()
         return 0
 
     lax.fori_loop(0, chunks, sent, 0)
@@ -373,15 +395,19 @@
     if fused:
         for k in range(1, pieces):
             peer = lax.rem(i + k, pieces)
-            remote(
-                spec.at[0, 0], regroup.at[peer], s_send.at[0, 0], s_recv.at[peer], {"bx": peer}
-            ).wait_recv()
+            for part in range(spans):
+                cols = pl.ds(part * span, span)
+                remote(
+                    spec.at[0, 0, :, cols], regroup.at[peer, :, cols], s_send.at[0, 0, part],
+                    s_recv.at[peer, part], {"bx": peer},
+                ).wait_recv()
         out_ref[...] = regroup[...]
         for c in range(chunks):
             for o in range(per):
                 @pl.when(owner(c, o) != i)
                 def _():
-                    regrouped(c, o).wait_send()
+                    for part in range(spans):
+                        regrouped(c, o, part).wait_send()
 
 
 def shards(source, start_tick, op_x, op_y):
@@ -403,9 +429,12 @@
     single = pltpu.VMEM((CHUNKS, rows, width), BF16)
     operator = pltpu.VMEM((2 * width, width), BF16)
     ticked_sem = pltpu.SemaphoreType.DMA((TICKS - 1, CHUNKS))
+    tiles = pl.cdiv(width, 256)
+    spans = 2 if tiles % 2 == 0 else 1
+    tiled_sem = pltpu.SemaphoreType.DMA((CHUNKS, tiles))
     single_sem = pltpu.SemaphoreType.DMA((CHUNKS,))
     result = pl.pallas_call(
-        functools.partial(kernel, (pieces, rows_by, per, group, fused)),
+        functools.partial(kernel, (pieces, rows_by, per, group, fused, spans)),
         out_shape=out_shape,
         in_specs=[pl.BlockSpec(memory_space=pltpu.SMEM)] + [pl.BlockSpec(memory_space=pl.ANY)] * 4,
         out_specs=pl.BlockSpec(memory_space=pltpu.VMEM),
@@ -418,12 +447,12 @@
             single, single, single, single, single,
             pltpu.VMEM((CHUNKS, per, 2 * group, width), BF16),
             pltpu.VMEM((pieces, 2 * group, width) if fused else (1, 16, 128), BF16),
-            pltpu.SemaphoreType.DMA((2 + 2 * pl.cdiv(width, 256),)),
+            pltpu.SemaphoreType.DMA((2 + 2 * tiles,)),
             ticked_sem, ticked_sem, ticked_sem, ticked_sem,
+            tiled_sem, tiled_sem, tiled_sem, tiled_sem,
             single_sem, single_sem, single_sem, single_sem,
-            single_sem, single_sem, single_sem, single_sem,
-            pltpu.SemaphoreType.DMA((CHUNKS, per)),
-            pltpu.SemaphoreType.DMA((pieces,)),
+            pltpu.SemaphoreType.DMA((CHUNKS, per, spans)),
+            pltpu.SemaphoreType.DMA((pieces, spans)),
         ],
         compiler_params=pltpu.CompilerParams(
             collective_id=0, has_side_effects=True, vmem_limit_bytes=60 * 1024 * 1024

time: 74 us -> 71.4 us (0.965)
  Pallas kernels: 70.8 us -> 68 us
    pallas_call x1, Pallas kernels: 70.8 us -> 68 us  [shards(): pl.pallas_call(functools.partial(kernel, (pieces, rows_by, per, group, fu...]
where the time goes in v2:
time: 71.4 us; the launch traced here: 71 us
  Pallas kernels  68 us (95%)
  matrix products  2.32 us (3%)
    pallas_call x1, Pallas kernels, shards(): pl.pallas_call(functools.partial(kernel, (pieces, rows_by, per, group, fu...  68 us
    dot_general x1, matrix products, shards(): jnp.dot(grid, result.reshape(side, width), preferred_element_type=F32)  2.32 us

profile of v2, /device:TPU:4, one launch (start us, length us, event | category | flops | bytes accessed | tf_op | source)
XLA Modules:
  0.0 71.0 jit_solution(4052165638714313794)
XLA Ops:
  0.7 0.0 copy-start
  0.7 0.0 copy-start.1
  0.7 68.0 %shard_map.73 = bf16[8,32,1024]{2,1,0:T(8,128)(2,1)} custom-call(s32[1,1]{1,0:T(1,128)S(6)} %copy.8.first_ref, bf16[2,128,1024]{2,1,0:T(8,128)(2,1)} %bitcast.12, bf16[2048,1024]{1,0:T(8,128)(2,1)} %bitcast.10, bf16[2048,1024]{1,0:T(8,128)(2,1)} %bitcast.11, bf16[2048,1024]{1,0:T(8,128)(2,1)} %constant.6.clone.tables_hbm), custom_call_target="tpu_custom_call" | custom-call | flops 10737418240 | bytes 16777216 | tf_op jit(solution)/shard_map/pallas_call | solution.py:436
  68.6 0.0 copy-done
  68.6 0.0 copy-done.1
  68.7 2.3 %convolution_multiply_fusion = f32[1024,256]{0,1:T(8,128)} fusion(bf16[256,256]{1,0:T(8,128)(2,1)S(1)} %copy-done, bf16[256,1024]{1,0:T(8,128)(2,1)} %bitcast.9, f32[256]{0:T(256)S(1)} %copy-done.1), kind=kOutput, calls=%fused_computation | convolution fusion | flops 134479872 | bytes 1704960 | tf_op jit(solution)/shard_map/dot_general | solution.py:473
Async XLA Ops:
  0.7 68.0 %copy-start = (bf16[256,256]{1,0:T(8,128)(2,1)S(1)}, bf16[256,256]{1,0:T(8,128)(2,1)}, u32[]{:S(2)}) copy-start(bf16[256,256]{1,0:T(8,128)(2,1)} %constant.7.clone) | copy-start | bytes 393220
  0.7 68.0 %copy-start.1 = (f32[256]{0:T(256)S(1)}, f32[256]{0:T(256)}, u32[]{:S(2)}) copy-start(f32[256]{0:T(256)} %constant.8.clone) | copy-start | bytes 3076

commit v3 on v2

--- a/solution.py
+++ b/solution.py
@@ -11,7 +11,7 @@
 from jax.sharding import PartitionSpec as P
 
 TICKS = 4
-CHUNKS = 2
+CHUNKS = 4
 MESH = pl.DeviceIdType.MESH
 BF16 = jnp.bfloat16
 F32 = jnp.float32

time: 71.4 us -> 73.4 us (1.028)
  the two profiles are of different devices: /device:TPU:4 before, /device:TPU:24 now
where the time goes in v3:
time: 73.4 us; the launch traced here: 73.2 us
  Pallas kernels  70.2 us (96%)
  matrix products  2.32 us (3%)
    pallas_call x1, Pallas kernels, shards(): pl.pallas_call(functools.partial(kernel, (pieces, rows_by, per, group, fu...  70.2 us
    dot_general x1, matrix products, shards(): jnp.dot(grid, result.reshape(side, width), preferred_element_type=F32)  2.32 us

profile of v3, /device:TPU:24, one launch (start us, length us, event | category | flops | bytes accessed | tf_op | source)
XLA Modules:
  0.0 73.2 jit_solution(4237268273729152513)
XLA Ops:
  0.7 0.0 copy-start
  0.7 0.0 copy-start.1
  0.7 70.2 %shard_map.73 = bf16[8,32,1024]{2,1,0:T(8,128)(2,1)} custom-call(s32[1,1]{1,0:T(1,128)S(6)} %copy.8.first_ref, bf16[2,128,1024]{2,1,0:T(8,128)(2,1)} %bitcast.12, bf16[2048,1024]{1,0:T(8,128)(2,1)} %bitcast.10, bf16[2048,1024]{1,0:T(8,128)(2,1)} %bitcast.11, bf16[2048,1024]{1,0:T(8,128)(2,1)} %constant.6.clone.tables_hbm), custom_call_target="tpu_custom_call" | custom-call | flops 10737418240 | bytes 16777216 | tf_op jit(solution)/shard_map/pallas_call | solution.py:436
  70.9 0.0 copy-done
  70.9 0.0 copy-done.1
  70.9 2.3 %convolution_multiply_fusion = f32[1024,256]{0,1:T(8,128)} fusion(bf16[256,256]{1,0:T(8,128)(2,1)S(1)} %copy-done, bf16[256,1024]{1,0:T(8,128)(2,1)} %bitcast.9, f32[256]{0:T(256)S(1)} %copy-done.1), kind=kOutput, calls=%fused_computation | convolution fusion | flops 134479872 | bytes 1704960 | tf_op jit(solution)/shard_map/dot_general | solution.py:473
Async XLA Ops:
  0.7 70.2 %copy-start = (bf16[256,256]{1,0:T(8,128)(2,1)S(1)}, bf16[256,256]{1,0:T(8,128)(2,1)}, u32[]{:S(2)}) copy-start(bf16[256,256]{1,0:T(8,128)(2,1)} %constant.7.clone) | copy-start | bytes 393220
  0.7 70.2 %copy-start.1 = (f32[256]{0:T(256)S(1)}, f32[256]{0:T(256)}, u32[]{:S(2)}) copy-start(f32[256]{0:T(256)} %constant.8.clone) | copy-start | bytes 3076

commit v4 on v2

--- a/solution.py
+++ b/solution.py
@@ -127,7 +127,6 @@
     lax.fori_loop(0, chunks, clear_all, 0)
 
     peers = pieces - 1 + (j > 0).astype(jnp.int32) + (j < rows_by - 1).astype(jnp.int32)
-    pl.semaphore_wait(barrier, peers)
 
     def remote(src, dst, send, recv, where):
         return pltpu.make_async_remote_copy(
@@ -232,6 +231,8 @@
             e_out[tick, c, :, cols] = value
 
         product(opx, put_east, opx_loads if first else None)
+        if first:
+            pl.semaphore_wait(barrier, peers)
 
         @pl.when(i < pieces - 1)
         def _():
@@ -255,7 +256,7 @@
     tables_load.wait()
     last = TICKS - 1
 
-    def last_tick(c):
+    def last_east(c):
         arrive(last, c)
         incident(last, c)
 
@@ -269,6 +270,7 @@
 
         product(opx, put_east, then=send_east)
 
+    def last_north(c):
         def put_north(cols, value):
             n_out[last, c, :, cols] = value
 
@@ -349,11 +351,15 @@
     def finish(step, _):
         @pl.when(step < chunks)
         def _():
-            last_tick(step)
+            last_east(step)
 
         @pl.when((step >= 1) & (step <= chunks))
         def _():
             subtract(step - 1)
+
+        @pl.when(step < chunks)
+        def _():
+            last_north(step)
 
         @pl.when(step >= 2)
         def _():

time: 71.4 us -> 70.3 us (0.985)
  Pallas kernels: 68 us -> 66.8 us
    pallas_call x1, Pallas kernels: 68 us -> 66.8 us  [shards(): pl.pallas_call(functools.partial(kernel, (pieces, rows_by, per, group, fu...]
where the time goes in v4:
time: 70.3 us; the launch traced here: 69.8 us
  Pallas kernels  66.8 us (95%)
  matrix products  2.32 us (3%)
    pallas_call x1, Pallas kernels, shards(): pl.pallas_call(functools.partial(kernel, (pieces, rows_by, per, group, fu...  66.8 us
    dot_general x1, matrix products, shards(): jnp.dot(grid, result.reshape(side, width), preferred_element_type=F32)  2.32 us

profile of v4, /device:TPU:4, one launch (start us, length us, event | category | flops | bytes accessed | tf_op | source)
XLA Modules:
  0.0 69.8 jit_solution(16541385643113267814)
XLA Ops:
  0.7 0.0 copy-start
  0.7 0.0 copy-start.1
  0.7 66.8 %shard_map.73 = bf16[8,32,1024]{2,1,0:T(8,128)(2,1)} custom-call(s32[1,1]{1,0:T(1,128)S(6)} %copy.8.first_ref, bf16[2,128,1024]{2,1,0:T(8,128)(2,1)} %bitcast.12, bf16[2048,1024]{1,0:T(8,128)(2,1)} %bitcast.10, bf16[2048,1024]{1,0:T(8,128)(2,1)} %bitcast.11, bf16[2048,1024]{1,0:T(8,128)(2,1)} %constant.6.clone.tables_hbm), custom_call_target="tpu_custom_call" | custom-call | flops 10737418240 | bytes 16777216 | tf_op jit(solution)/shard_map/pallas_call | solution.py:442
  67.5 0.0 copy-done
  67.5 0.0 copy-done.1
  67.5 2.3 %convolution_multiply_fusion = f32[1024,256]{0,1:T(8,128)} fusion(bf16[256,256]{1,0:T(8,128)(2,1)S(1)} %copy-done, bf16[256,1024]{1,0:T(8,128)(2,1)} %bitcast.9, f32[256]{0:T(256)S(1)} %copy-done.1), kind=kOutput, calls=%fused_computation | convolution fusion | flops 134479872 | bytes 1704960 | tf_op jit(solution)/shard_map/dot_general | solution.py:479
Async XLA Ops:
  0.7 66.8 %copy-start = (bf16[256,256]{1,0:T(8,128)(2,1)S(1)}, bf16[256,256]{1,0:T(8,128)(2,1)}, u32[]{:S(2)}) copy-start(bf16[256,256]{1,0:T(8,128)(2,1)} %constant.7.clone) | copy-start | bytes 393220
  0.7 66.8 %copy-start.1 = (f32[256]{0:T(256)S(1)}, f32[256]{0:T(256)}, u32[]{:S(2)}) copy-start(f32[256]{0:T(256)} %constant.8.clone) | copy-start | bytes 3076

commit v5 on v4

--- a/solution.py
+++ b/solution.py
@@ -133,9 +133,11 @@
             src_ref=src, dst_ref=dst, send_sem=send, recv_sem=recv, device_id=where, device_id_type=MESH
         )
 
-    def east(tick, c):
+    def east(tick, c, part):
+        cols = pl.ds(part * span, span)
         return remote(
-            e_out.at[tick, c], e_in.at[tick + 1, c], e_send.at[tick, c], e_recv.at[tick, c], {"bx": i + 1}
+            e_out.at[tick, c, :, cols], e_in.at[tick + 1, c, :, cols], e_send.at[tick, c, part],
+            e_recv.at[tick, c, part], {"bx": i + 1},
         )
 
     def north(tick, c):
@@ -211,7 +213,8 @@
     def arrive(tick, c):
         @pl.when(i > 0)
         def _():
-            east(tick - 1, c).wait_recv()
+            for part in range(spans):
+                east(tick - 1, c, part).wait_recv()
 
         @pl.when(j > 0)
         def _():
@@ -230,13 +233,18 @@
         def put_east(cols, value):
             e_out[tick, c, :, cols] = value
 
-        product(opx, put_east, opx_loads if first else None)
-        if first:
-            pl.semaphore_wait(barrier, peers)
-
-        @pl.when(i < pieces - 1)
-        def _():
-            east(tick, c).start()
+        def send_east(n):
+            if (n + 1) * spans % count:
+                return
+            part = (n + 1) * spans // count - 1
+            if first and part == 0:
+                pl.semaphore_wait(barrier, peers)
+
+            @pl.when(i < pieces - 1)
+            def _():
+                east(tick, c, part).start()
+
+        product(opx, put_east, opx_loads if first else None, send_east)
 
         def put_north(cols, value):
             n_out[tick, c, :, cols] = value
@@ -373,7 +381,8 @@
         for tick in range(TICKS - 1):
             @pl.when(i < pieces - 1)
             def _():
-                east(tick, c).wait_send()
+                for part in range(spans):
+                    east(tick, c, part).wait_send()
 
             @pl.when(j < rows_by - 1)
             def _():
@@ -437,6 +446,7 @@
     ticked_sem = pltpu.SemaphoreType.DMA((TICKS - 1, CHUNKS))
     tiles = pl.cdiv(width, 256)
     spans = 2 if tiles % 2 == 0 else 1
+    halved_sem = pltpu.SemaphoreType.DMA((TICKS - 1, CHUNKS, spans))
     tiled_sem = pltpu.SemaphoreType.DMA((CHUNKS, tiles))
     single_sem = pltpu.SemaphoreType.DMA((CHUNKS,))
     result = pl.pallas_call(
@@ -454,7 +464,7 @@
             pltpu.VMEM((CHUNKS, per, 2 * group, width), BF16),
             pltpu.VMEM((pieces, 2 * group, width) if fused else (1, 16, 128), BF16),
             pltpu.SemaphoreType.DMA((2 + 2 * tiles,)),
-            ticked_sem, ticked_sem, ticked_sem, ticked_sem,
+            halved_sem, halved_sem, ticked_sem, ticked_sem,
             tiled_sem, tiled_sem, tiled_sem, tiled_sem,
             single_sem, single_sem, single_sem, single_sem,
             pltpu.SemaphoreType.DMA((CHUNKS, per, spans)),

time: 70.3 us -> 69.2 us (0.984)
  Pallas kernels: 66.8 us -> 65.7 us
    pallas_call x1, Pallas kernels: 66.8 us -> 65.7 us  [shards(): pl.pallas_call(functools.partial(kernel, (pieces, rows_by, per, group, fu...]
where the time goes in v5:
time: 69.2 us; the launch traced here: 68.7 us
  Pallas kernels  65.7 us (95%)
  matrix products  2.32 us (3%)
    pallas_call x1, Pallas kernels, shards(): pl.pallas_call(functools.partial(kernel, (pieces, rows_by, per, group, fu...  65.7 us
    dot_general x1, matrix products, shards(): jnp.dot(grid, result.reshape(side, width), preferred_element_type=F32)  2.32 us

profile of v5, /device:TPU:4, one launch (start us, length us, event | category | flops | bytes accessed | tf_op | source)
XLA Modules:
  0.0 68.7 jit_solution(11879005807490955144)
XLA Ops:
  0.7 0.0 copy-start
  0.7 0.0 copy-start.1
  0.7 65.7 %shard_map.73 = bf16[8,32,1024]{2,1,0:T(8,128)(2,1)} custom-call(s32[1,1]{1,0:T(1,128)S(6)} %copy.8.first_ref, bf16[2,128,1024]{2,1,0:T(8,128)(2,1)} %bitcast.12, bf16[2048,1024]{1,0:T(8,128)(2,1)} %bitcast.10, bf16[2048,1024]{1,0:T(8,128)(2,1)} %bitcast.11, bf16[2048,1024]{1,0:T(8,128)(2,1)} %constant.6.clone.tables_hbm), custom_call_target="tpu_custom_call" | custom-call | flops 10737418240 | bytes 16777216 | tf_op jit(solution)/shard_map/pallas_call | solution.py:452
  66.4 0.0 copy-done
  66.4 0.0 copy-done.1
  66.4 2.3 %convolution_multiply_fusion = f32[1024,256]{0,1:T(8,128)} fusion(bf16[256,256]{1,0:T(8,128)(2,1)S(1)} %copy-done, bf16[256,1024]{1,0:T(8,128)(2,1)} %bitcast.9, f32[256]{0:T(256)S(1)} %copy-done.1), kind=kOutput, calls=%fused_computation | convolution fusion | flops 134479872 | bytes 1704960 | tf_op jit(solution)/shard_map/dot_general | solution.py:489
Async XLA Ops:
  0.7 65.8 %copy-start = (bf16[256,256]{1,0:T(8,128)(2,1)S(1)}, bf16[256,256]{1,0:T(8,128)(2,1)}, u32[]{:S(2)}) copy-start(bf16[256,256]{1,0:T(8,128)(2,1)} %constant.7.clone) | copy-start | bytes 393220
  0.7 65.8 %copy-start.1 = (f32[256]{0:T(256)S(1)}, f32[256]{0:T(256)}, u32[]{:S(2)}) copy-start(f32[256]{0:T(256)} %constant.8.clone) | copy-start | bytes 3076
